TPU v7x, 256 devices: a whole 4x4x8 slice. The times are simulated.
256 devices in a mesh: tok: 16 (over z, core), exp: 16 (over y, x).
Axes of the slice: x: 4, y: 4, z: 8, core: 2. Of those that a mesh axis runs over, the one named last changes fastest.
Arguments:
- tokens: bfloat16 [131072, 2048], P(('tok', 'exp')), may hold values from -40 to 40
- first_factor: bfloat16 [128, 2048, 256], P('exp'), may hold values from -0.125 to 0.125
- expert_ids: int32 [131072, 8], P(('tok', 'exp')), may hold values from 0 to 127, all different within a row; in each aligned block of 512 rows (0 to 511, 512 to 1023, ...) at most 40 rows name the same one
Outputs:
- codes: bfloat16 [131072, 8, 256], P(('tok', 'exp'))
- upper_factor: float32 [128, 256, 256], P('exp')
Inputs may be any that keep to these rules, and one draw needn't show every extreme that they name: `expert_ids`: within the rows of one device (aligned blocks of 512 tokens) no expert is named more than 40 times, a bound that some block reaches; each token names 8 different experts, and every expert is named by some token.
All inputs are finite; a program needn't handle non-finite values.
Results may differ from a plain program's by a relative error of at most 0.0058.
Values may be sent and summed in bfloat16 or wider, within the bound.
No kernel may reach another device: no remote copies, remote signals or barrier semaphores. Data moves between devices by JAX's collectives and lax.ppermute only.
A program may use at most 256 MiB of HBM per device.

v0:
```python
import functools

import jax
import jax.numpy as jnp
from jax import lax
from jax.experimental import pallas as pl
from jax.experimental.pallas import tpu as pltpu
from jax.sharding import Mesh
from jax.sharding import PartitionSpec as P

RIDGE = 0.1
BLOCK = 64
SIDE = 4
NEAR = (0, -1, 1, 2)
WHOLE = pl.BlockSpec(memory_space=pltpu.VMEM)
SCALARS = pl.BlockSpec(memory_space=pltpu.SMEM)


def params(mebibytes):
    return pltpu.CompilerParams(vmem_limit_bytes=mebibytes * 2**20)


def exact_dot(a, b, dims):
    return lax.dot_general(
        a, b, (dims, ((), ())), precision=lax.Precision.HIGHEST, preferred_element_type=jnp.float32
    )


def dot(a, b):
    return jnp.dot(a, b, preferred_element_type=jnp.float32)


def shift(array, axis, step):
    size = lax.axis_size(axis)
    return lax.ppermute(array, axis, [(i, (i + step) % size) for i in range(size)])


def select_kernel(rank_ref, first_ref, *rest, capacity):
    *second_refs, out_ref, picks = rest
    experts, tok_rows = rank_ref.shape[1:]

    @pl.when(pl.program_id(0) == 0)
    def _():
        slots = lax.broadcasted_iota(jnp.int32, (capacity, tok_rows), 0).astype(jnp.float32)
        for source in range(2):
            for pair in range(experts // 2):
                both = [
                    jnp.where(rank_ref[source, e : e + 1, :] == slots, 1.0, 0.0)
                    for e in (2 * pair, 2 * pair + 1)
                ]
                picks[source, pair * 2 * capacity : (pair + 1) * 2 * capacity, :] = jnp.concatenate(
                    both, axis=0
                ).astype(jnp.bfloat16)

    blocks = (first_ref[...], jnp.concatenate([r[...] for r in second_refs], axis=0))
    step = 8
    for e in range(0, experts, step):
        rows = slice(e * capacity, (e + step) * capacity)
        found = [dot(picks[source, rows, :], blocks[source]) for source in range(2)]
        for i in range(step):
            own = slice(i * capacity, (i + 1) * capacity)
            out_ref[e + i] = jnp.concatenate([found[0][own], found[1][own]], axis=0).astype(
                out_ref.dtype
            )


def select(ranks, first, second, capacity, width, columns=512):
    _, experts, tok_rows = ranks.shape
    columns = min(columns, width)
    return pl.pallas_call(
        functools.partial(select_kernel, capacity=capacity),
        grid=(width // columns,),
        in_specs=[pl.BlockSpec(ranks.shape, lambda i: (0, 0, 0))]
        + [pl.BlockSpec((a.shape[0], columns), lambda i: (0, i)) for a in (first, *second)],
        out_specs=pl.BlockSpec((experts, 2 * capacity, columns), lambda i: (0, 0, i)),
        out_shape=jax.ShapeDtypeStruct((experts, 2 * capacity, width), first.dtype),
        scratch_shapes=[pltpu.VMEM((2, experts * capacity, tok_rows), jnp.bfloat16)],
        compiler_params=params(48),
        cost_estimate=pl.CostEstimate(
            flops=4 * experts * capacity * tok_rows * width, bytes_accessed=2**24, transcendentals=0
        ),
        name="select",
    )(ranks, first, *second)


def project_own_kernel(at_ref, near_ref, far_ref, factor_ref, out_ref):
    for i in range(out_ref.shape[0]):
        rows = jnp.concatenate([near_ref[i], far_ref[i]], axis=0)
        out_ref[i] = dot(rows, factor_ref[i]).astype(out_ref.dtype)


def project_kernel(at_ref, near_ref, far_ref, shared_ref, mine_ref, other_ref, out_ref):
    slices, _, _, thin, rank_k = shared_ref.shape
    half = mine_ref.shape[1]
    depth = slices * thin
    first = at_ref[1] == 0
    for i in range(out_ref.shape[0]):
        rows = jnp.concatenate([near_ref[i], far_ref[i]], axis=0)
        low, high = rows[:, depth : depth + half], rows[:, depth + half :]
        total = dot(rows[:, :depth], shared_ref[:, 0, i].reshape(depth, rank_k))
        total += dot(jnp.where(first, low, high), mine_ref[i])
        total += dot(jnp.where(first, high, low), other_ref[i])
        out_ref[i] = total.astype(out_ref.dtype)


def project(at, near, far, factors, per_group, start, count, index=None, step=2):
    width = near.shape[2]
    rank_k = factors[0].shape[-1]
    row_spec = lambda rows: pl.BlockSpec(
        (step, rows, width), lambda i, at: ((at[0] * per_group + start) // step + i, 0, 0)
    )
    plain = lambda a: pl.BlockSpec((step,) + a.shape[1:], lambda i, at: (i, 0, 0))
    if index is None:
        kernel, specs = project_own_kernel, [plain(factors[0])]
    else:
        shared = factors[0]
        kernel = project_kernel
        specs = [
            pl.BlockSpec(
                (shared.shape[0], 1, step) + shared.shape[3:],
                lambda i, at: (0, index, start // step + i, 0, 0),
            ),
            plain(factors[1]),
            plain(factors[2]),
        ]
    rows = near.shape[1] + far.shape[1]
    return pl.pallas_call(
        kernel,
        grid_spec=pltpu.PrefetchScalarGridSpec(
            num_scalar_prefetch=1,
            grid=(count // step,),
            in_specs=[row_spec(near.shape[1]), row_spec(far.shape[1])] + specs,
            out_specs=pl.BlockSpec((step, rows, rank_k), lambda i, at: (i, 0, 0)),
        ),
        out_shape=jax.ShapeDtypeStruct((count, rows, rank_k), near.dtype),
        compiler_params=params(48),
        cost_estimate=pl.CostEstimate(
            flops=2 * count * rows * width * rank_k,
            bytes_accessed=2 * count * width * (rows + rank_k),
            transcendentals=0,
        ),
        name="project",
    )(at, near, far, *factors)


def gram_kernel(at_ref, *refs, scale):
    *row_refs, mine_ref, other_ref = refs
    count, _, half, _ = mine_ref.shape
    core = at_ref[2]
    for out_ref, turn in ((mine_ref, core), (other_ref, 1 - core)):
        for i in range(count):
            rows = jnp.concatenate([r[turn * count + i] for r in row_refs], axis=0)
            lower, upper = rows[:, :half], rows[:, half:]
            transposed = ((0,), (0,))
            pairs = ((lower, lower), (lower, upper), (upper, upper))
            for block, (a, b) in enumerate(pairs):
                out_ref[i, block] = scale * lax.dot_general(
                    a, b, (transposed, ((), ())), preferred_element_type=jnp.float32
                )


def partial_grams(at, rows, scale):
    experts, _, rank_k = rows[0].shape
    half = jax.ShapeDtypeStruct((experts // 2, 3, rank_k // 2, rank_k // 2), jnp.float32)
    return pl.pallas_call(
        functools.partial(gram_kernel, scale=scale),
        in_specs=[SCALARS] + [WHOLE] * len(rows),
        out_specs=(WHOLE, WHOLE),
        out_shape=(half, half),
        compiler_params=params(16),
        name="grams",
    )(at, *rows)


def factor_kernel(gram_ref, upper_ref, inverse_ref, work, *, block):
    experts, _, half, _ = gram_ref.shape
    size = 2 * half
    lanes = 128
    groups = lanes // block
    tiles = experts // groups
    rows_h = lax.broadcasted_iota(jnp.int32, (half, half), 0)
    cols_h = lax.broadcasted_iota(jnp.int32, (half, half), 1)
    ridge_h = jnp.where(rows_h == cols_h, RIDGE, 0.0).astype(jnp.float32)
    for e in range(experts):
        work[e, :half, :half] = gram_ref[e, 0] + ridge_h
        work[e, :half, half:] = gram_ref[e, 1]
        work[e, half:, half:] = gram_ref[e, 2] + ridge_h
    lane = lax.broadcasted_iota(jnp.int32, (block, lanes), 1)
    row = lax.broadcasted_iota(jnp.int32, (block, lanes), 0)
    unit = jnp.where(lane % block == row, 1.0, 0.0).astype(jnp.float32)
    base = (lane // block) * block
    for k in range(size // block):
        lo, hi = k * block, (k + 1) * block
        packed = [
            jnp.concatenate([work[t * groups + g, lo:hi, lo:hi] for g in range(groups)], axis=1)
            for t in range(tiles)
        ]
        inverse = [unit for _ in range(tiles)]
        scales = [jnp.ones((block, lanes), jnp.float32) for _ in range(tiles)]
        for j in range(0, block, 4):
            for t in range(tiles):
                s, n = packed[t], inverse[t]
                columns = [
                    jnp.take_along_axis(s, base + (j + i), axis=1, mode="promise_in_bounds")
                    for i in range(4)
                ]
                heads = [s[j + i : j + i + 1, :] for i in range(4)]
                tails = [n[j + i : j + i + 1, :] for i in range(4)]
                for i in range(4):
                    at = j + i
                    root = lax.rsqrt(columns[i][at : at + 1, :])
                    inv = root * root
                    scales[t] = jnp.where(row == at, root, scales[t])
                    factor = jnp.where(row > at, columns[i] * inv, 0.0)
                    for m in range(i + 1, 4):
                        ratio = columns[m][at : at + 1, :] * inv
                        columns[m] = columns[m] - columns[i] * ratio
                    s = s - factor * heads[i]
                    n = n - factor * tails[i]
                    for m in range(i + 1, 4):
                        ratio = factor[j + m : j + m + 1, :]
                        heads[m] = heads[m] - ratio * heads[i]
                        tails[m] = tails[m] - ratio * tails[i]
                packed[t], inverse[t] = s, n
        packed = [jnp.where(lane % block >= row, s * c, 0.0) for s, c in zip(packed, scales)]
        inverse = [n * c for n, c in zip(inverse, scales)]
        for e in range(experts):
            t, g = e // groups, e % groups
            work[e, lo:hi, lo:hi] = jnp.eye(block, dtype=jnp.float32)
            strip = exact_dot(
                inverse[t][:, g * block : (g + 1) * block], work[e, lo:hi, :], ((1,), (0,))
            )
            if lo:
                upper_ref[e, lo:hi, :lo] = jnp.zeros((block, lo), jnp.float32)
            upper_ref[e, lo:hi, lo:hi] = packed[t][:, g * block : (g + 1) * block]
            work[e, lo:hi, :] = strip
            if hi < size:
                upper_ref[e, lo:hi, hi:] = strip[:, hi:]
                work[e, hi:, lo:hi] = jnp.zeros((size - hi, block), jnp.float32)
                work[e, hi:, :] = work[e, hi:, :] - exact_dot(strip[:, hi:], strip, ((0,), (0,)))
    rows = lax.broadcasted_iota(jnp.int32, (size, size), 0)
    cols = lax.broadcasted_iota(jnp.int32, (size, size), 1)
    for e in range(experts):
        whole = jnp.where(rows >= cols, work[e], 0.0)
        high = whole.astype(jnp.bfloat16)
        inverse_ref[0, e] = high
        inverse_ref[1, e] = (whole - high.astype(jnp.float32)).astype(jnp.bfloat16)


def factorize(grams):
    experts, _, half, _ = grams.shape
    square = (experts, 2 * half, 2 * half)
    return pl.pallas_call(
        functools.partial(factor_kernel, block=BLOCK),
        in_specs=[WHOLE],
        out_specs=(WHOLE, WHOLE),
        out_shape=(
            jax.ShapeDtypeStruct(square, jnp.float32),
            jax.ShapeDtypeStruct((2,) + square, jnp.bfloat16),
        ),
        scratch_shapes=[pltpu.VMEM(square, jnp.float32)],
        compiler_params=params(24),
        name="factorize",
    )(grams)


def whiten_kernel(at_ref, mine_ref, other_ref, *refs, capacity):
    *row_refs, codes_ref = refs
    count = mine_ref.shape[1]
    y, x, core = at_ref[0], at_ref[1], at_ref[2]
    across = (((1,), (1,)), ((), ()))
    terms = [
        [
            jnp.where(core == e // count, mine_ref[term, e % count], other_ref[term, e % count])
            for term in range(2)
        ]
        for e in range(2 * count)
    ]
    for away, rows_ref in zip((0, 1, -1, 2), row_refs):
        found = [
            sum(
                lax.dot_general(rows_ref[e], term, across, preferred_element_type=jnp.float32)
                for term in terms[e]
            )
            for e in range(2 * count)
        ]
        for i, step in enumerate(NEAR):
            owner = lax.rem(y + step + SIDE, SIDE) * SIDE + lax.rem(x + away + SIDE, SIDE)
            own = slice(i * capacity, (i + 1) * capacity)
            codes_ref[owner] = jnp.concatenate([f[own] for f in found], axis=0).astype(
                codes_ref.dtype
            )


def whiten(at, mine, other, rows, capacity):
    _, count, size, _ = mine.shape
    return pl.pallas_call(
        functools.partial(whiten_kernel, capacity=capacity),
        in_specs=[SCALARS] + [WHOLE] * (2 + len(rows)),
        out_specs=WHOLE,
        out_shape=jax.ShapeDtypeStruct((SIDE * SIDE, 2 * count * capacity, size), jnp.bfloat16),
        compiler_params=params(56),
        name="whiten",
    )(at, mine, other, *rows)


def place_kernel(slot_ref, rows_ref, out_ref, *, width):
    tokens, top_k = slot_ref.shape
    count = tokens * top_k
    spread = jnp.broadcast_to(slot_ref[...][:, None, :], (tokens, top_k, top_k))
    lane = lax.broadcasted_iota(jnp.int32, (count, top_k), 1)
    row = lax.broadcasted_iota(jnp.int32, (count, top_k), 0)
    own = jnp.where(lane == row % top_k, spread.reshape(count, top_k), 0.0)
    slot = jnp.sum(own, axis=1, keepdims=True)
    column = lax.broadcasted_iota(jnp.int32, (count, width), 1).astype(jnp.float32)
    total = jnp.zeros(out_ref.shape, jnp.float32)
    for first in range(0, rows_ref.shape[0], width):
        pick = jnp.where(slot - float(first) == column, 1.0, 0.0).astype(rows_ref.dtype)
        total += dot(pick, rows_ref[first : first + width, :])
    out_ref[...] = total.astype(out_ref.dtype)


def place(slot, rows, step=128, width=512):
    tokens, top_k = slot.shape
    return pl.pallas_call(
        functools.partial(place_kernel, width=width),
        grid=(tokens // step,),
        in_specs=[
            pl.BlockSpec((step, top_k), lambda i: (i, 0)),
            pl.BlockSpec(rows.shape, lambda i: (0, 0)),
        ],
        out_specs=pl.BlockSpec((step * top_k, rows.shape[1]), lambda i: (i, 0)),
        out_shape=jax.ShapeDtypeStruct((tokens * top_k, rows.shape[1]), rows.dtype),
        compiler_params=params(40),
        name="place",
    )(slot, rows)


def slot_ranks(ids, first, experts):
    blocks, rows, _ = ids.shape
    wanted = first + jnp.arange(experts, dtype=jnp.int32)
    named = (jnp.swapaxes(ids, 1, 2)[:, :, None, :] == wanted[None, None, :, None]).any(axis=1)
    later = jnp.arange(rows)[:, None] < jnp.arange(rows)[None, :]
    rank = dot(named.reshape(-1, rows).astype(jnp.bfloat16), later.astype(jnp.bfloat16))
    return jnp.where(named, rank.reshape(named.shape), -1.0)


def sum_over_tok(mine, other):
    shape = mine.shape
    lanes = shape[-1]
    layers = lax.axis_size("z")
    mine = mine + shift(other, "c", 1)
    pieces = lax.all_to_all(mine.reshape(layers, -1, lanes), "z", 0, 0, tiled=True)
    return lax.all_gather(jnp.sum(pieces, axis=0), "z", tiled=True).reshape(shape)


def local(tokens, first_factor, expert_ids):
    groups = lax.axis_size(("y", "x"))
    tok_ranks = lax.axis_size(("z", "c"))
    per_group, model_dim, rank_k = first_factor.shape
    tok_rows, top_k = expert_ids.shape
    experts = groups * per_group
    capacity = tok_rows * top_k * 5 // (4 * experts)
    gram_scale = experts / (top_k * tok_rows * tok_ranks * groups)
    y, x, core = lax.axis_index("y"), lax.axis_index("x"), lax.axis_index("c")
    at = jnp.stack([y, x, core]).astype(jnp.int32)

    depth = model_dim // 2
    thin = depth // tok_ranks
    thick = depth // 2
    middle = per_group // 2
    half_rows = tok_rows // 2
    tied = lax.optimization_barrier
    lanes = 128
    tagged = jnp.concatenate(
        [tokens, jnp.pad(expert_ids.astype(tokens.dtype), ((0, 0), (0, lanes - top_k)))], axis=1
    )
    slices = lax.dynamic_slice_in_dim(first_factor, lax.axis_index(("z", "c")) * thin, thin, 1)
    thick_slice = lax.dynamic_slice_in_dim(first_factor, depth + core * thick, thick, 1)
    slices_before, slices_after, slices_far = shift(slices, "x", 1), shift(slices, "x", -1), shift(slices, "x", 2)
    tagged, thick_slice, slices_before, slices_after, slices_far = tied(
        (tagged, thick_slice, slices_before, slices_after, slices_far)
    )
    shared = lax.all_gather(jnp.stack([slices_before, slices_after, slices_far]), ("z", "c"))
    tokens_before, tokens_after, mine_before, mine_after = tied(
        (
            shift(tagged, "y", 1),
            shift(tagged, "y", -1),
            shift(thick_slice, "x", 1),
            shift(thick_slice, "x", -1),
        )
    )
    tokens_far = [shift(tokens_before[:half_rows], "y", 1), shift(tokens_after[half_rows:], "y", -1)]
    mine_far = [shift(mine_before[:middle], "x", 1), shift(mine_after[middle:], "x", -1)]
    ids_of = lambda a: a[:, model_dim : model_dim + top_k].astype(jnp.int32)
    first_of = y * SIDE * per_group
    near_ids = jnp.stack([expert_ids, ids_of(tokens_before)])
    near = select(
        slot_ranks(near_ids, first_of, SIDE * per_group),
        tokens,
        [tokens_before],
        capacity,
        model_dim,
    )
    near, *tokens_far = tied((near, *tokens_far))
    far_ids = jnp.stack(
        [ids_of(tokens_after), jnp.concatenate([ids_of(a) for a in tokens_far], axis=0)]
    )
    far = select(
        slot_ranks(far_ids, first_of, SIDE * per_group),
        tokens_after,
        tokens_far,
        capacity,
        model_dim,
    )
    far, mine_before, mine_after, *mine_far = tied((far, mine_before, mine_after, *mine_far))
    other_far = [shift(a, "c", 1) for a in mine_far]
    mine_before, mine_after, *other_far = tied((mine_before, mine_after, *other_far))
    other_before, other_after = shift(mine_before, "c", 1), shift(mine_after, "c", 1)

    def projected(step, factors, start, count, index=None):
        where = jnp.stack([(x + step) % SIDE, core]).astype(jnp.int32)
        return project(where, near, far, factors, per_group, start, count, index)

    to_far = [
        projected(2, [shared, mine_far[i], other_far[i]], i * middle, middle, 2) for i in range(2)
    ]
    near, far, *to_far = tied((near, far, *to_far))
    from_far = [shift(shift(a, "x", way), "x", way) for a, way in zip(to_far, (1, -1))]
    to_before = projected(-1, [shared, mine_before, other_before], 0, per_group, 0)
    near, far, to_before = tied((near, far, to_before))
    from_after = shift(to_before, "x", -1)
    to_after = projected(1, [shared, mine_after, other_after], 0, per_group, 1)
    near, far, to_after = tied((near, far, to_after))
    from_before = shift(to_after, "x", 1)
    rows_own = projected(0, [first_factor], 0, per_group)
    rows_own, expert_ids = tied((rows_own, expert_ids))
    from_far = jnp.concatenate(from_far, axis=0)
    rows = [rows_own, from_after, from_before, from_far]

    upper, inverse = factorize(sum_over_tok(*partial_grams(at, rows, gram_scale)))
    codes = whiten(at, inverse, shift(inverse, "c", 1), rows, capacity)
    upper, codes = tied((upper, codes))
    returned = lax.all_to_all(codes, ("y", "x"), 0, 0, tiled=True)
    other = shift(upper, "c", 1)
    upper = jnp.where(
        core == 0, jnp.concatenate([upper, other]), jnp.concatenate([other, upper])
    )

    own_ranks = slot_ranks(expert_ids[None], 0, experts)[0]
    named = expert_ids.T[:, None, :] == jnp.arange(experts, dtype=jnp.int32)[None, :, None]
    slot = (expert_ids.T * capacity).astype(jnp.float32) + jnp.sum(
        jnp.where(named, own_ranks, 0.0), axis=1
    )
    gathered = place(slot.T, returned.reshape(experts * capacity, rank_k))
    return (gathered.reshape(tok_rows, top_k, rank_k), upper)


def solution(mesh):
    fine = Mesh(mesh.devices.reshape(-1, 2, SIDE, SIDE), ("z", "c", "y", "x"))
    every = ("z", "c", "y", "x")
    in_specs = (P(every, None), P(("y", "x"), None, None), P(every, None))
    out_specs = (P(every, None, None), P(("y", "x"), None, None))
    return jax.shard_map(local, mesh=fine, in_specs=in_specs, out_specs=out_specs, check_vma=False)
```

profile of v0, /device:TPU:1, one launch (start us, length us, event | category | flops | bytes accessed | tf_op | source)
XLA Modules:
  0.0 337.6 jit_solution(14502982661361999020)
XLA Ops:
  14.2 3.2 fusion.1
  17.4 3.0 constant_dynamic-slice_fusion.1
  20.4 3.7 %collective-permute-done.2 = bf16[8,64,256]{2,1,0:T(8,128)(2,1)S(1)} collective-permute-done((bf16[8,64,256]{2,1,0:T(8,128)(2,1)S(1)}, bf16[8,64,256]{2,1,0:T(8,128)(2,1)S(1)}, u32[]{:S(2)}, u32[]{:S(2)}) %collective-permute-start.2) | collective-permute-done | bytes 262176 | tf_op jit(solution)/shard_map/ppermute | solution.py:35
  30.7 44.0 %collective-permute-done.5.mine_ref = bf16[8,512,256]{2,1,0:T(8,128)(2,1)} collective-permute-done((bf16[8,512,256]{2,1,0:T(8,128)(2,1)}, bf16[8,512,256]{2,1,0:T(8,128)(2,1)}, u32[]{:S(2)}, u32[]{:S(2)}) %collective-permute-start.5) | collective-permute-done | bytes 2097184 | tf_op jit(solution)/shard_map/ppermute | solution.py:35
  75.2 2.3 slice.25
  78.6 2.3 slice.26
  83.7 2.5 slice.30
  87.5 2.7 collective-permute-start.10
  90.6 9.4 %select.15.near_ref = bf16[32,80,2048]{2,1,0:T(8,128)(2,1)} custom-call(f32[2,32,512]{2,1,0:T(8,128)S(1)} %convolution_select_fusion.2.rank_ref, bf16[512,2048]{1,0:T(8,128)(2,1)S(1)} %copy-done.4, bf16[512,2176]{1,0:T(8,128)(2,1)} %collective-permute-done.3.rest_0_), custom_call_target="tpu_custom_call" | custom-call | flops 5368709120 | bytes 16777216 | tf_op jit(solution)/shard_map/select/pallas_call | solution.py:70
  100.0 2.7 collective-permute-done.7.rest_0_
  106.5 9.9 %select.16.far_ref = bf16[32,80,2048]{2,1,0:T(8,128)(2,1)} custom-call(f32[2,32,512]{2,1,0:T(8,128)S(1)} %convolution_select_fusion.1.rank_ref, bf16[512,2176]{1,0:T(8,128)(2,1)} %collective-permute-done.4.first_ref, bf16[256,2176]{1,0:T(8,128)(2,1)} %collective-permute-done.7.rest_0_, bf16[256,2176]{1,0:T(8,128)(2,1)} %collective-permute-done.8.rest_1_), custom_call_target="tpu_custom_call" | custom-call | flops 5368709120 | bytes 16777216 | tf_op jit(solution)/shard_map/select/pallas_call | solution.py:70
  116.4 4.0 %collective-permute-start.11 = (bf16[4,512,256]{2,1,0:T(8,128)(2,1)S(1)}, bf16[4,512,256]{2,1,0:T(8,128)(2,1)S(1)}, u32[]{:S(2)}, u32[]{:S(2)}) collective-permute-start(bf16[4,512,256]{2,1,0:T(8,128)(2,1)S(1)} %collective-permute-done.9.mine_ref), channel_id=1, source_target_pairs={{0,16},{16,0},{1,17},{17,1},{2,18},{18,2},{3,19},{19,3},{4,20},{20... | collective-permute-start | bytes 3145736 | tf_op jit(solution)/shard_map/ppermute | solution.py:35
  120.6 2.7 collective-permute-done.11.other_ref
  127.3 4.1 %project.5 = bf16[4,160,256]{2,1,0:T(8,128)(2,1)} custom-call(s32[2]{0:T(128)S(1)} %pad_add_fusion.1.at_ref, bf16[32,80,2048]{2,1,0:T(8,128)(2,1)} %select.15.near_ref, bf16[32,80,2048]{2,1,0:T(8,128)(2,1)} %select.16.far_ref, bf16[16,3,8,64,256]{4,3,2,1,0:T(8,128)(2,1)} %bitcast.44, bf16[4,512,256]{2,1,0:T(8,128)(2,1)S(1)} %collective-permute-done.9.mine_ref, ...), custom_call_target="tpu_custom_call" | custom-call | flops 671088640 | bytes 6815744 | tf_op jit(solution)/shard_map/project/pallas_call | solution.py:127
  131.4 4.4 %project.6 = bf16[4,160,256]{2,1,0:T(8,128)(2,1)} custom-call(s32[2]{0:T(128)S(1)} %pad_add_fusion.1.at_ref, bf16[32,80,2048]{2,1,0:T(8,128)(2,1)} %select.15.near_ref, bf16[32,80,2048]{2,1,0:T(8,128)(2,1)} %select.16.far_ref, bf16[16,3,8,64,256]{4,3,2,1,0:T(8,128)(2,1)} %bitcast.45, bf16[4,512,256]{2,1,0:T(8,128)(2,1)} %collective-permute-done.10.mine_ref, ...), custom_call_target="tpu_custom_call" | custom-call | flops 671088640 | bytes 6815744 | tf_op jit(solution)/shard_map/project/pallas_call | solution.py:127
  136.1 2.5 collective-permute-start.19
  138.6 6.7 %project.7 = bf16[8,160,256]{2,1,0:T(8,128)(2,1)S(1)} custom-call(s32[2]{0:T(128)S(1)} %pad_add_fusion.2.at_ref, bf16[32,80,2048]{2,1,0:T(8,128)(2,1)} %select.15.near_ref, bf16[32,80,2048]{2,1,0:T(8,128)(2,1)} %select.16.far_ref, bf16[16,3,8,64,256]{4,3,2,1,0:T(8,128)(2,1)} %bitcast.46, bf16[8,512,256]{2,1,0:T(8,128)(2,1)} %collective-permute-done.5.mine_ref, ...), custom_call_target="tpu_custom_call" | custom-call | flops 1342177280 | bytes 13631488 | tf_op jit(solution)/shard_map/project/pallas_call | solution.py:127
  145.3 6.2 %project.8 = bf16[8,160,256]{2,1,0:T(8,128)(2,1)S(1)} custom-call(s32[2]{0:T(128)S(1)} %pad_add_fusion.3.at_ref, bf16[32,80,2048]{2,1,0:T(8,128)(2,1)} %select.15.near_ref, bf16[32,80,2048]{2,1,0:T(8,128)(2,1)} %select.16.far_ref, bf16[16,3,8,64,256]{4,3,2,1,0:T(8,128)(2,1)} %bitcast.47, bf16[8,512,256]{2,1,0:T(8,128)(2,1)S(1)} %collective-permute-done.6.mine_ref, ...), custom_call_target="tpu_custom_call" | custom-call | flops 1342177280 | bytes 13631488 | tf_op jit(solution)/shard_map/project/pallas_call | solution.py:127
  153.2 2.7 collective-permute-start.20
  156.0 6.9 %project.9.refs_0_ = bf16[8,160,256]{2,1,0:T(8,128)(2,1)S(1)} custom-call(s32[2]{0:T(128)S(1)} %pad_add_fusion.at_ref, bf16[32,80,2048]{2,1,0:T(8,128)(2,1)} %select.15.near_ref, bf16[32,80,2048]{2,1,0:T(8,128)(2,1)} %select.16.far_ref, bf16[8,2048,256]{2,1,0:T(8,128)(2,1)} %factor_ref.1), custom_call_target="tpu_custom_call" | custom-call | flops 1342177280 | bytes 13631488 | tf_op jit(solution)/shard_map/project/pallas_call | solution.py:127
  162.9 12.2 %collective-permute-done.18 = bf16[4,160,256]{2,1,0:T(8,128)(2,1)S(1)} collective-permute-done((bf16[4,160,256]{2,1,0:T(8,128)(2,1)}, bf16[4,160,256]{2,1,0:T(8,128)(2,1)S(1)}, u32[]{:S(2)}, u32[]{:S(2)}) %collective-permute-start.18) | collective-permute-done | bytes 327712 | tf_op jit(solution)/shard_map/ppermute | solution.py:35
  176.9 2.2 collective-permute-start.21
  181.2 30.3 %all_to_all.10 = f32[8,192,128]{2,1,0:T(8,128)S(1)} all-to-all(f32[8,192,128]{2,1,0:T(8,128)S(1)} %bitcast.48), channel_id=1, replica_groups=mesh['z'=8,'c'=2,'y'=4,'x'=4] {'z'}, dimensions={0} | all-to-all | bytes 1572864 | tf_op jit(solution)/shard_map/all_to_all | solution.py:353
  211.6 29.4 %all_gather.11 = f32[1536,128]{1,0:T(8,128)S(1)} all-gather(f32[192,128]{1,0:T(8,128)S(1)} %reduce_sum.22), channel_id=1, replica_groups=mesh['z'=8,'c'=2,'y'=4,'x'=4] {'z'}, dimensions={0}, use_global_device_ids=true | all-gather | bytes 884736 | tf_op jit(solution)/shard_map/all_gather | solution.py:354
  241.0 14.2 %factorize.1 = (f32[4,256,256]{2,1,0:T(8,128)S(1)}, bf16[2,4,256,256]{3,2,1,0:T(8,128)(2,1)S(1)}) custom-call(f32[4,3,128,128]{3,2,1,0:T(8,128)S(1)} %bitcast.43), custom_call_target="tpu_custom_call" | custom-call | tf_op jit(solution)/shard_map/factorize/pallas_call | solution.py:253
  256.2 7.1 %collective-permute-start.22 = (bf16[2,4,256,256]{3,2,1,0:T(8,128)(2,1)S(1)}, bf16[2,4,256,256]{3,2,1,0:T(8,128)(2,1)S(1)}, u32[]{:S(2)}, u32[]{:S(2)}) collective-permute-start(bf16[2,4,256,256]{3,2,1,0:T(8,128)(2,1)S(1)} %get-tuple-element.77.mine_ref), channel_id=1, source_target_pairs={{0,16},{16,0},{1,17},{17,1},{2,18},{18,2},{3,19},{19,3},{4,20},{20... | collective-permute-start | bytes 3145736 | tf_op jit(solution)/shard_map/ppermute | solution.py:35
  263.3 2.3 collective-permute-done.22.other_ref
  266.6 6.8 %whiten.1 = bf16[16,320,256]{2,1,0:T(8,128)(2,1)} custom-call(s32[3]{0:T(128)} %copy-done.11, bf16[2,4,256,256]{3,2,1,0:T(8,128)(2,1)} %copy-done.10, bf16[2,4,256,256]{3,2,1,0:T(8,128)(2,1)} %copy-done.12, bf16[8,160,256]{2,1,0:T(8,128)(2,1)} %copy-done, bf16[8,160,256]{2,1,0:T(8,128)(2,1)} %copy-done.2, bf16[8,160,256]{2,1,0:T(8,128)(2,1)} %copy-done.3, ...), custom_call_target="tpu_custom_call" | custom-call | tf_op jit(solution)/shard_map/whiten/pallas_call | solution.py:297
  273.4 4.8 %all-to-all-start.1 = ((bf16[16,320,256]{2,1,0:T(8,128)(2,1)}), bf16[16,320,256]{2,1,0:T(8,128)(2,1)S(1)}, u32[]{:S(2)}, u32[]{:S(2)}) async-start(bf16[16,320,256]{2,1,0:T(8,128)(2,1)} %whiten.1), calls=%async_computation.1 | async-start | bytes 5242880 | tf_op jit(solution)/shard_map/all_to_all | solution.py:444
  281.5 4.0 %maximum_select_fusion = f32[8,256,256]{2,1,0:T(8,128)} fusion(f32[4,256,256]{2,1,0:T(8,128)} %collective-permute-done.23, f32[4,256,256]{2,1,0:T(8,128)} %copy-done.9, pred[]{:T(512)S(6)} %eq.81), kind=kLoop, calls=%fused_computation.3 | loop fusion | flops 1572864 | bytes 4194305 | tf_op jit(solution)/shard_map/jit(_where)/select_n | solution.py:446
  285.5 32.4 %all-to-all-done.1 = bf16[16,320,256]{2,1,0:T(8,128)(2,1)S(1)} async-done(((bf16[16,320,256]{2,1,0:T(8,128)(2,1)}), bf16[16,320,256]{2,1,0:T(8,128)(2,1)S(1)}, u32[]{:S(2)}, u32[]{:S(2)}) %all-to-all-start.1) | async-done | bytes 2621472 | tf_op jit(solution)/shard_map/all_to_all | solution.py:444
  317.9 12.6 %place.1 = bf16[4096,256]{1,0:T(8,128)(2,1)} custom-call(f32[512,8]{1,0:T(8,128)S(1)} %bitcast_add_fusion.slot_ref, bf16[5120,256]{1,0:T(8,128)(2,1)S(1)} %bitcast.42), custom_call_target="tpu_custom_call" | custom-call | tf_op jit(solution)/shard_map/place/pallas_call | solution.py:325
  (104 shorter events, 38.7 us)
Async XLA Ops:
  7.2 118.9 %all-gather.3.cloned.1.call-start = ((), (), s32[]{:S(2)}) async-start(), calls=%async_computation.2 | async-start | bytes 13369344 | tf_op jit(solution)/shard_map/all_gather | solution.py:384
  8.2 12.2 %collective-permute-start = (bf16[8,64,256]{2,1,0:T(8,128)(2,1)S(1)}, bf16[8,64,256]{2,1,0:T(8,128)(2,1)S(1)}, u32[]{:S(2)}, u32[]{:S(2)}) collective-permute-start(bf16[8,64,256]{2,1,0:T(8,128)(2,1)S(1)} %constant_dynamic-slice_fusion), channel_id=1, source_target_pairs={{0,1},{1,2},{2,3},{3,0},{4,5},{5,6},{6,7},{7,4},{8,9},{9,10},{10,1... | collective-permute-start | bytes 786440 | tf_op jit(solution)/shard_map/ppermute | solution.py:35
  10.3 10.1 %collective-permute-start.1 = (bf16[8,64,256]{2,1,0:T(8,128)(2,1)S(1)}, bf16[8,64,256]{2,1,0:T(8,128)(2,1)S(1)}, u32[]{:S(2)}, u32[]{:S(2)}) collective-permute-start(bf16[8,64,256]{2,1,0:T(8,128)(2,1)S(1)} %constant_dynamic-slice_fusion), channel_id=1, source_target_pairs={{0,3},{1,0},{2,1},{3,2},{4,7},{5,4},{6,5},{7,6},{8,11},{9,8},{10,9... | collective-permute-start | bytes 786440 | tf_op jit(solution)/shard_map/ppermute | solution.py:35
  11.7 12.4 %collective-permute-start.2 = (bf16[8,64,256]{2,1,0:T(8,128)(2,1)S(1)}, bf16[8,64,256]{2,1,0:T(8,128)(2,1)S(1)}, u32[]{:S(2)}, u32[]{:S(2)}) collective-permute-start(bf16[8,64,256]{2,1,0:T(8,128)(2,1)S(1)} %constant_dynamic-slice_fusion), channel_id=1, source_target_pairs={{0,2},{1,3},{2,0},{3,1},{4,6},{5,7},{6,4},{7,5},{8,10},{9,11},{10,... | collective-permute-start | bytes 786440 | tf_op jit(solution)/shard_map/ppermute | solution.py:35
  25.1 50.1 %collective-permute-start.3 = (bf16[512,2176]{1,0:T(8,128)(2,1)}, bf16[512,2176]{1,0:T(8,128)(2,1)}, u32[]{:S(2)}, u32[]{:S(2)}) collective-permute-start(bf16[512,2176]{1,0:T(8,128)(2,1)} %fusion.1), channel_id=1, source_target_pairs={{0,4},{4,8},{8,12},{12,0},{1,5},{5,9},{9,13},{13,1},{2,6},{6,10},{... | collective-permute-start | bytes 6684680 | tf_op jit(solution)/shard_map/ppermute | solution.py:35
  26.5 48.7 %collective-permute-start.4 = (bf16[512,2176]{1,0:T(8,128)(2,1)}, bf16[512,2176]{1,0:T(8,128)(2,1)}, u32[]{:S(2)}, u32[]{:S(2)}) collective-permute-start(bf16[512,2176]{1,0:T(8,128)(2,1)} %fusion.1), channel_id=1, source_target_pairs={{0,12},{4,0},{8,4},{12,8},{1,13},{5,1},{9,5},{13,9},{2,14},{6,2},{... | collective-permute-start | bytes 6684680 | tf_op jit(solution)/shard_map/ppermute | solution.py:35
  28.0 46.7 %collective-permute-start.5 = (bf16[8,512,256]{2,1,0:T(8,128)(2,1)}, bf16[8,512,256]{2,1,0:T(8,128)(2,1)}, u32[]{:S(2)}, u32[]{:S(2)}) collective-permute-start(bf16[8,512,256]{2,1,0:T(8,128)(2,1)} %constant_dynamic-slice_fusion.1), channel_id=1, source_target_pairs={{0,1},{1,2},{2,3},{3,0},{4,5},{5,6},{6,7},{7,4},{8,9},{9,10},{10,1... | collective-permute-start | bytes 6291464 | tf_op jit(solution)/shard_map/ppermute | solution.py:35
  28.5 46.2 %collective-permute-start.6 = (bf16[8,512,256]{2,1,0:T(8,128)(2,1)}, bf16[8,512,256]{2,1,0:T(8,128)(2,1)S(1)}, u32[]{:S(2)}, u32[]{:S(2)}) collective-permute-start(bf16[8,512,256]{2,1,0:T(8,128)(2,1)} %constant_dynamic-slice_fusion.1), channel_id=1, source_target_pairs={{0,3},{1,0},{2,1},{3,2},{4,7},{5,4},{6,5},{7,6},{8,11},{9,8},{10,9... | collective-permute-start | bytes 6291464 | tf_op jit(solution)/shard_map/ppermute | solution.py:35
  77.5 25.2 %collective-permute-start.7 = (bf16[256,2176]{1,0:T(8,128)(2,1)}, bf16[256,2176]{1,0:T(8,128)(2,1)}, u32[]{:S(2)}, u32[]{:S(2)}) collective-permute-start(bf16[256,2176]{1,0:T(8,128)(2,1)} %slice.25), channel_id=1, source_target_pairs={{0,4},{4,8},{8,12},{12,0},{1,5},{5,9},{9,13},{13,1},{2,6},{6,10},{... | collective-permute-start | bytes 3342344 | tf_op jit(solution)/shard_map/ppermute | solution.py:35
  80.9 23.4 %collective-permute-start.8 = (bf16[256,2176]{1,0:T(8,128)(2,1)}, bf16[256,2176]{1,0:T(8,128)(2,1)}, u32[]{:S(2)}, u32[]{:S(2)}) collective-permute-start(bf16[256,2176]{1,0:T(8,128)(2,1)} %slice.26), channel_id=1, source_target_pairs={{0,12},{4,0},{8,4},{12,8},{1,13},{5,1},{9,5},{13,9},{2,14},{6,2},{... | collective-permute-start | bytes 3342344 | tf_op jit(solution)/shard_map/ppermute | solution.py:35
  83.7 6.5 %copy-start.13 = (s32[512,8]{0,1:T(8,128)S(1)}, s32[512,8]{0,1:T(8,128)}, u32[]{:S(2)}) copy-start(s32[512,8]{0,1:T(8,128)} %param.5) | copy-start | bytes 49156
  83.7 6.9 %copy-start.4 = (bf16[512,2048]{1,0:T(8,128)(2,1)S(1)}, bf16[512,2048]{1,0:T(8,128)(2,1)}, u32[]{:S(2)}) copy-start(bf16[512,2048]{1,0:T(8,128)(2,1)} %first_ref.1) | copy-start | bytes 6291460
  86.2 30.2 %collective-permute-start.9 = (bf16[4,512,256]{2,1,0:T(8,128)(2,1)}, bf16[4,512,256]{2,1,0:T(8,128)(2,1)S(1)}, u32[]{:S(2)}, u32[]{:S(2)}) collective-permute-start(bf16[4,512,256]{2,1,0:T(8,128)(2,1)} %slice.30), channel_id=1, source_target_pairs={{0,1},{1,2},{2,3},{3,0},{4,5},{5,6},{6,7},{7,4},{8,9},{9,10},{10,1... | collective-permute-start | bytes 3145736 | tf_op jit(solution)/shard_map/ppermute | solution.py:35
  87.5 28.9 %collective-permute-start.10 = (bf16[4,512,256]{2,1,0:T(8,128)(2,1)}, bf16[4,512,256]{2,1,0:T(8,128)(2,1)}, u32[]{:S(2)}, u32[]{:S(2)}) collective-permute-start(bf16[4,512,256]{2,1,0:T(8,128)(2,1)} %slice.31), channel_id=1, source_target_pairs={{0,3},{1,0},{2,1},{3,2},{4,7},{5,4},{6,5},{7,6},{8,11},{9,8},{10,9... | collective-permute-start | bytes 3145736 | tf_op jit(solution)/shard_map/ppermute | solution.py:35
  116.4 6.8 %collective-permute-start.11 = (bf16[4,512,256]{2,1,0:T(8,128)(2,1)S(1)}, bf16[4,512,256]{2,1,0:T(8,128)(2,1)S(1)}, u32[]{:S(2)}, u32[]{:S(2)}) collective-permute-start(bf16[4,512,256]{2,1,0:T(8,128)(2,1)S(1)} %collective-permute-done.9.mine_ref), channel_id=1, source_target_pairs={{0,16},{16,0},{1,17},{17,1},{2,18},{18,2},{3,19},{19,3},{4,20},{20... | collective-permute-start | bytes 3145736 | tf_op jit(solution)/shard_map/ppermute | solution.py:35
  120.5 4.0 %collective-permute-start.12 = (bf16[4,512,256]{2,1,0:T(8,128)(2,1)}, bf16[4,512,256]{2,1,0:T(8,128)(2,1)S(1)}, u32[]{:S(2)}, u32[]{:S(2)}) collective-permute-start(bf16[4,512,256]{2,1,0:T(8,128)(2,1)} %collective-permute-done.10.mine_ref), channel_id=1, source_target_pairs={{0,16},{16,0},{1,17},{17,1},{2,18},{18,2},{3,19},{19,3},{4,20},{20... | collective-permute-start | bytes 3145736 | tf_op jit(solution)/shard_map/ppermute | solution.py:35
  125.4 13.2 %collective-permute-start.13 = (bf16[8,512,256]{2,1,0:T(8,128)(2,1)}, bf16[8,512,256]{2,1,0:T(8,128)(2,1)}, u32[]{:S(2)}, u32[]{:S(2)}) collective-permute-start(bf16[8,512,256]{2,1,0:T(8,128)(2,1)} %collective-permute-done.5.mine_ref), channel_id=1, source_target_pairs={{0,16},{16,0},{1,17},{17,1},{2,18},{18,2},{3,19},{19,3},{4,20},{20... | collective-permute-start | bytes 6291464 | tf_op jit(solution)/shard_map/ppermute | solution.py:35
  125.8 19.5 %collective-permute-start.14 = (bf16[8,512,256]{2,1,0:T(8,128)(2,1)S(1)}, bf16[8,512,256]{2,1,0:T(8,128)(2,1)}, u32[]{:S(2)}, u32[]{:S(2)}) collective-permute-start(bf16[8,512,256]{2,1,0:T(8,128)(2,1)S(1)} %collective-permute-done.6.mine_ref), channel_id=1, source_target_pairs={{0,16},{16,0},{1,17},{17,1},{2,18},{18,2},{3,19},{19,3},{4,20},{20... | collective-permute-start | bytes 6291464 | tf_op jit(solution)/shard_map/ppermute | solution.py:35
  135.8 17.3 %collective-permute-start.17 = (bf16[4,160,256]{2,1,0:T(8,128)(2,1)}, bf16[4,160,256]{2,1,0:T(8,128)(2,1)}, u32[]{:S(2)}, u32[]{:S(2)}) collective-permute-start(bf16[4,160,256]{2,1,0:T(8,128)(2,1)} %project.5), channel_id=1, source_target_pairs={{0,1},{1,2},{2,3},{3,0},{4,5},{5,6},{6,7},{7,4},{8,9},{9,10},{10,1... | collective-permute-start | bytes 983048 | tf_op jit(solution)/shard_map/ppermute | solution.py:35
  136.1 17.2 %collective-permute-start.19 = (bf16[4,160,256]{2,1,0:T(8,128)(2,1)}, bf16[4,160,256]{2,1,0:T(8,128)(2,1)}, u32[]{:S(2)}, u32[]{:S(2)}) collective-permute-start(bf16[4,160,256]{2,1,0:T(8,128)(2,1)} %project.6), channel_id=1, source_target_pairs={{0,3},{1,0},{2,1},{3,2},{4,7},{5,4},{6,5},{7,6},{8,11},{9,8},{10,9... | collective-permute-start | bytes 983048 | tf_op jit(solution)/shard_map/ppermute | solution.py:35
  151.6 23.6 %collective-permute-start.15 = (bf16[8,160,256]{2,1,0:T(8,128)(2,1)S(1)}, bf16[8,160,256]{2,1,0:T(8,128)(2,1)S(1)}, u32[]{:S(2)}, u32[]{:S(2)}) collective-permute-start(bf16[8,160,256]{2,1,0:T(8,128)(2,1)S(1)} %project.7), channel_id=1, source_target_pairs={{0,3},{1,0},{2,1},{3,2},{4,7},{5,4},{6,5},{7,6},{8,11},{9,8},{10,9... | collective-permute-start | bytes 1966088 | tf_op jit(solution)/shard_map/ppermute | solution.py:35
  151.8 23.3 %collective-permute-start.16 = (bf16[8,160,256]{2,1,0:T(8,128)(2,1)S(1)}, bf16[8,160,256]{2,1,0:T(8,128)(2,1)S(1)}, u32[]{:S(2)}, u32[]{:S(2)}) collective-permute-start(bf16[8,160,256]{2,1,0:T(8,128)(2,1)S(1)} %project.8), channel_id=1, source_target_pairs={{0,1},{1,2},{2,3},{3,0},{4,5},{5,6},{6,7},{7,4},{8,9},{9,10},{10,1... | collective-permute-start | bytes 1966088 | tf_op jit(solution)/shard_map/ppermute | solution.py:35
  153.1 21.9 %collective-permute-start.18 = (bf16[4,160,256]{2,1,0:T(8,128)(2,1)}, bf16[4,160,256]{2,1,0:T(8,128)(2,1)S(1)}, u32[]{:S(2)}, u32[]{:S(2)}) collective-permute-start(bf16[4,160,256]{2,1,0:T(8,128)(2,1)} %collective-permute-done.17), channel_id=1, source_target_pairs={{0,1},{1,2},{2,3},{3,0},{4,5},{5,6},{6,7},{7,4},{8,9},{9,10},{10,1... | collective-permute-start | bytes 983048 | tf_op jit(solution)/shard_map/ppermute | solution.py:35
  153.2 21.8 %collective-permute-start.20 = (bf16[4,160,256]{2,1,0:T(8,128)(2,1)}, bf16[4,160,256]{2,1,0:T(8,128)(2,1)S(1)}, u32[]{:S(2)}, u32[]{:S(2)}) collective-permute-start(bf16[4,160,256]{2,1,0:T(8,128)(2,1)} %collective-permute-done.19), channel_id=1, source_target_pairs={{0,3},{1,0},{2,1},{3,2},{4,7},{5,4},{6,5},{7,6},{8,11},{9,8},{10,9... | collective-permute-start | bytes 983048 | tf_op jit(solution)/shard_map/ppermute | solution.py:35
  156.0 19.2 %copy-start.11 = (s32[3]{0:T(128)}, s32[3]{0:T(128)S(1)}, u32[]{:S(2)}) copy-start(s32[3]{0:T(128)S(1)} %pad_add_fusion.4.at_ref) | copy-start | bytes 40
  162.9 18.3 %copy-start = (bf16[8,160,256]{2,1,0:T(8,128)(2,1)}, bf16[8,160,256]{2,1,0:T(8,128)(2,1)S(1)}, u32[]{:S(2)}) copy-start(bf16[8,160,256]{2,1,0:T(8,128)(2,1)S(1)} %project.9.refs_0_) | copy-start | bytes 1966084
  175.1 6.1 %copy-start.1 = (bf16[8,160,256]{2,1,0:T(8,128)(2,1)}, bf16[8,160,256]{2,1,0:T(8,128)(2,1)S(1)}, u32[]{:S(2)}) copy-start(bf16[8,160,256]{2,1,0:T(8,128)(2,1)S(1)} %constant_dynamic-update-slice_fusion.refs_3_) | copy-start | bytes 1966084
  176.9 4.1 %collective-permute-start.21 = (f32[4,3,128,128]{3,2,1,0:T(8,128)S(1)}, f32[4,3,128,128]{3,2,1,0:T(8,128)S(1)}, u32[]{:S(2)}, u32[]{:S(2)}) collective-permute-start(f32[4,3,128,128]{3,2,1,0:T(8,128)S(1)} %get-tuple-element.75), channel_id=1, source_target_pairs={{0,16},{16,0},{1,17},{17,1},{2,18},{18,2},{3,19},{19,3},{4,20},{20... | collective-permute-start | bytes 2359304 | tf_op jit(solution)/shard_map/ppermute | solution.py:35
  256.2 9.4 %copy-start.10 = (bf16[2,4,256,256]{3,2,1,0:T(8,128)(2,1)}, bf16[2,4,256,256]{3,2,1,0:T(8,128)(2,1)S(1)}, u32[]{:S(2)}) copy-start(bf16[2,4,256,256]{3,2,1,0:T(8,128)(2,1)S(1)} %get-tuple-element.77.mine_ref) | copy-start | bytes 3145732
  256.2 9.4 %collective-permute-start.22 = (bf16[2,4,256,256]{3,2,1,0:T(8,128)(2,1)S(1)}, bf16[2,4,256,256]{3,2,1,0:T(8,128)(2,1)S(1)}, u32[]{:S(2)}, u32[]{:S(2)}) collective-permute-start(bf16[2,4,256,256]{3,2,1,0:T(8,128)(2,1)S(1)} %get-tuple-element.77.mine_ref), channel_id=1, source_target_pairs={{0,16},{16,0},{1,17},{17,1},{2,18},{18,2},{3,19},{19,3},{4,20},{20... | collective-permute-start | bytes 3145736 | tf_op jit(solution)/shard_map/ppermute | solution.py:35
  273.4 44.6 %all-to-all-start.1 = ((bf16[16,320,256]{2,1,0:T(8,128)(2,1)}), bf16[16,320,256]{2,1,0:T(8,128)(2,1)S(1)}, u32[]{:S(2)}, u32[]{:S(2)}) async-start(bf16[16,320,256]{2,1,0:T(8,128)(2,1)} %whiten.1), calls=%async_computation.1 | async-start | bytes 5242880 | tf_op jit(solution)/shard_map/all_to_all | solution.py:444
  278.2 3.4 collective-permute-start.23
  (8 other events, 21.3 us)
Sparse Core Ops, SparseCore 0:
  25.2 78.8 all-gather.2
where the time goes:
time: 341 us; the launch traced here: 338 us
  waiting for transfers between devices  106 us (31%)
  Pallas kernels  82.9 us (24%)
  blocking collectives  59.7 us (18%)
  starting transfers between devices  42.8 us (13%)
  local copies, waits for them, and re-layouts  19.8 us (6%)
  between operations  14.6 us (4%)
  other arithmetic  11.3 us (3%)
    ppermute x24, waiting for transfers between devices, shift(): lax.ppermute(array, axis, [(i, (i + step) % size) for i in range(size)])  73.3 us
    ppermute x24, starting transfers between devices, shift(): lax.ppermute(array, axis, [(i, (i + step) % size) for i in range(size)])  37.9 us
    all_to_all x1, waiting for transfers between devices, local(): returned = lax.all_to_all(codes, ('y', 'x'), 0, 0, tiled=True)  32.4 us
    all_to_all x1, blocking collectives, sum_over_tok(): lax.all_to_all(mine.reshape(layers, -1, lanes), 'z', 0, 0, tiled=True)  30.3 us
    all_gather x1, blocking collectives, sum_over_tok(): lax.all_gather(jnp.sum(pieces, axis=0), 'z', tiled=True).reshape(shape)  29.4 us
    pallas_call x5, Pallas kernels, project(): pl.pallas_call(kernel, grid_spec=pltpu.PrefetchScalarGridSpec(num_scalar_...  28.3 us
    pallas_call x2, Pallas kernels, select(): pl.pallas_call(functools.partial(select_kernel, capacity=capacity), grid=...  19.3 us
    pallas_call x1, Pallas kernels, factorize(): pl.pallas_call(functools.partial(factor_kernel, block=BLOCK), in_specs=[W...  14.2 us
  transfers between devices with their start and end apart: 26, of which 12 were waited for; matrix products, arithmetic and copies ran while one was open for 7% of the time, Pallas kernels for 14%

commit v1 on v0

--- a/solution.py
+++ b/solution.py
@@ -299,7 +299,7 @@
         in_specs=[SCALARS] + [WHOLE] * (2 + len(rows)),
         out_specs=WHOLE,
         out_shape=jax.ShapeDtypeStruct((SIDE * SIDE, 2 * count * capacity, size), jnp.bfloat16),
-        compiler_params=params(56),
+        compiler_params=params(24),
         name="whiten",
     )(at, mine, other, *rows)
 
@@ -365,9 +365,9 @@
     y, x, core = lax.axis_index("y"), lax.axis_index("x"), lax.axis_index("c")
     at = jnp.stack([y, x, core]).astype(jnp.int32)
 
-    depth = model_dim // 2
+    depth = model_dim * 5 // 8
     thin = depth // tok_ranks
-    thick = depth // 2
+    thick = (model_dim - depth) // 2
     middle = per_group // 2
     half_rows = tok_rows // 2
     tied = lax.optimization_barrier
@@ -382,12 +382,15 @@
         (tagged, thick_slice, slices_before, slices_after, slices_far)
     )
     shared = lax.all_gather(jnp.stack([slices_before, slices_after, slices_far]), ("z", "c"))
-    tokens_before, tokens_after, mine_before, mine_after = tied(
+    mine_before, mine_after = tied((shift(thick_slice, "x", 1), shift(thick_slice, "x", -1)))
+    tokens_before, tokens_after, mine_before, mine_after, other_before, other_after = tied(
         (
             shift(tagged, "y", 1),
             shift(tagged, "y", -1),
-            shift(thick_slice, "x", 1),
-            shift(thick_slice, "x", -1),
+            mine_before,
+            mine_after,
+            shift(mine_before, "c", 1),
+            shift(mine_after, "c", 1),
         )
     )
     tokens_far = [shift(tokens_before[:half_rows], "y", 1), shift(tokens_after[half_rows:], "y", -1)]
@@ -402,7 +405,9 @@
         capacity,
         model_dim,
     )
-    near, *tokens_far = tied((near, *tokens_far))
+    near, *arrived = tied((near, *tokens_far, *mine_far))
+    tokens_far, mine_far = arrived[:2], arrived[2:]
+    other_far = [shift(a, "c", 1) for a in mine_far]
     far_ids = jnp.stack(
         [ids_of(tokens_after), jnp.concatenate([ids_of(a) for a in tokens_far], axis=0)]
     )
@@ -413,10 +418,7 @@
         capacity,
         model_dim,
     )
-    far, mine_before, mine_after, *mine_far = tied((far, mine_before, mine_after, *mine_far))
-    other_far = [shift(a, "c", 1) for a in mine_far]
-    mine_before, mine_after, *other_far = tied((mine_before, mine_after, *other_far))
-    other_before, other_after = shift(mine_before, "c", 1), shift(mine_after, "c", 1)
+    far, *other_far = tied((far, *other_far))
 
     def projected(step, factors, start, count, index=None):
         where = jnp.stack([(x + step) % SIDE, core]).astype(jnp.int32)

time: 341 us -> 343 us (level)
    unnamed x29 -> x25, local copies, waits for them, and re-layouts: 5.16 us -> 7.04 us
  transfers between devices with their start and end apart: 26 -> 26, of which waited for: 12 -> 12; matrix products, arithmetic and copies ran while one was open for 7% -> 6% of each run, Pallas kernels for 14% -> 12%
where the time goes in v1:
time: 343 us; the launch traced here: 339 us
  waiting for transfers between devices  109 us (32%)
  Pallas kernels  80.9 us (24%)
  blocking collectives  59.8 us (17%)
  starting transfers between devices  45.2 us (13%)
  local copies, waits for them, and re-layouts  20.5 us (6%)
  between operations  14.5 us (4%)
  other arithmetic  8.86 us (3%)
    ppermute x24, waiting for transfers between devices, shift(): lax.ppermute(array, axis, [(i, (i + step) % size) for i in range(size)])  76.2 us
    ppermute x24, starting transfers between devices, shift(): lax.ppermute(array, axis, [(i, (i + step) % size) for i in range(size)])  40.8 us
    all_to_all x1, waiting for transfers between devices, local(): returned = lax.all_to_all(codes, ('y', 'x'), 0, 0, tiled=True)  32.6 us
    all_to_all x1, blocking collectives, sum_over_tok(): lax.all_to_all(mine.reshape(layers, -1, lanes), 'z', 0, 0, tiled=True)  30.3 us
    all_gather x1, blocking collectives, sum_over_tok(): lax.all_gather(jnp.sum(pieces, axis=0), 'z', tiled=True).reshape(shape)  29.4 us
    pallas_call x5, Pallas kernels, project(): pl.pallas_call(kernel, grid_spec=pltpu.PrefetchScalarGridSpec(num_scalar_...  29.4 us
    pallas_call x2, Pallas kernels, select(): pl.pallas_call(functools.partial(select_kernel, capacity=capacity), grid=...  19.5 us
    pallas_call x1, Pallas kernels, factorize(): pl.pallas_call(functools.partial(factor_kernel, block=BLOCK), in_specs=[W...  14.2 us
  transfers between devices with their start and end apart: 26, of which 12 were waited for; matrix products, arithmetic and copies ran while one was open for 6% of the time, Pallas kernels for 12%

profile of v1, /device:TPU:1, one launch (start us, length us, event | category | flops | bytes accessed | tf_op | source)
XLA Modules:
  0.0 339.2 jit_solution(16366479836160705231)
XLA Ops:
  13.5 2.7 constant_dynamic-slice_fusion.1
  18.4 8.7 %collective-permute-done.2 = bf16[8,80,256]{2,1,0:T(8,128)(2,1)S(1)} collective-permute-done((bf16[8,80,256]{2,1,0:T(8,128)(2,1)S(1)}, bf16[8,80,256]{2,1,0:T(8,128)(2,1)S(1)}, u32[]{:S(2)}, u32[]{:S(2)}) %collective-permute-start.2) | collective-permute-done | bytes 327712 | tf_op jit(solution)/shard_map/ppermute | solution.py:35
  28.6 2.3 collective-permute-start.6
  33.7 30.5 %collective-permute-done.5.mine_ref = bf16[8,384,256]{2,1,0:T(8,128)(2,1)S(1)} collective-permute-done((bf16[8,384,256]{2,1,0:T(8,128)(2,1)}, bf16[8,384,256]{2,1,0:T(8,128)(2,1)S(1)}, u32[]{:S(2)}, u32[]{:S(2)}) %collective-permute-start.5) | collective-permute-done | bytes 1572896 | tf_op jit(solution)/shard_map/ppermute | solution.py:35
  64.1 2.4 collective-permute-start.7
  66.6 13.8 %collective-permute-done.3.rest_0_ = bf16[512,2176]{1,0:T(8,128)(2,1)} collective-permute-done((bf16[512,2176]{1,0:T(8,128)(2,1)}, bf16[512,2176]{1,0:T(8,128)(2,1)}, u32[]{:S(2)}, u32[]{:S(2)}) %collective-permute-start.3) | collective-permute-done | bytes 2228256 | tf_op jit(solution)/shard_map/ppermute | solution.py:35
  80.4 2.4 slice.26
  82.8 2.3 collective-permute-start.10
  85.1 2.3 slice.25
  91.1 2.9 collective-permute-start.12
  96.2 9.4 %select.15.near_ref = bf16[32,80,2048]{2,1,0:T(8,128)(2,1)} custom-call(f32[2,32,512]{2,1,0:T(8,128)S(1)} %convolution_select_fusion.2.rank_ref, bf16[512,2048]{1,0:T(8,128)(2,1)S(1)} %copy-done.2, bf16[512,2176]{1,0:T(8,128)(2,1)} %collective-permute-done.3.rest_0_), custom_call_target="tpu_custom_call" | custom-call | flops 5368709120 | bytes 16777216 | tf_op jit(solution)/shard_map/select/pallas_call | solution.py:70
  107.4 4.1 %collective-permute-done.9.rest_0_ = bf16[256,2176]{1,0:T(8,128)(2,1)} collective-permute-done((bf16[256,2176]{1,0:T(8,128)(2,1)}, bf16[256,2176]{1,0:T(8,128)(2,1)}, u32[]{:S(2)}, u32[]{:S(2)}) %collective-permute-start.9) | collective-permute-done | bytes 1114144 | tf_op jit(solution)/shard_map/ppermute | solution.py:35
  113.3 4.5 %collective-permute-start.13 = (bf16[4,384,256]{2,1,0:T(8,128)(2,1)}, bf16[4,384,256]{2,1,0:T(8,128)(2,1)S(1)}, u32[]{:S(2)}, u32[]{:S(2)}) collective-permute-start(bf16[4,384,256]{2,1,0:T(8,128)(2,1)} %collective-permute-done.11.mine_ref), channel_id=1, source_target_pairs={{0,16},{16,0},{1,17},{17,1},{2,18},{18,2},{3,19},{19,3},{4,20},{20... | collective-permute-start | bytes 2359304 | tf_op jit(solution)/shard_map/ppermute | solution.py:35
  118.4 10.0 %select.16.far_ref = bf16[32,80,2048]{2,1,0:T(8,128)(2,1)} custom-call(f32[2,32,512]{2,1,0:T(8,128)S(1)} %convolution_select_fusion.1.rank_ref, bf16[512,2176]{1,0:T(8,128)(2,1)} %collective-permute-done.4.first_ref, bf16[256,2176]{1,0:T(8,128)(2,1)} %collective-permute-done.9.rest_0_, bf16[256,2176]{1,0:T(8,128)(2,1)} %collective-permute-done.10.rest_1_), custom_call_target="tpu_custom_call" | custom-call | flops 5368709120 | bytes 16777216 | tf_op jit(solution)/shard_map/select/pallas_call | solution.py:70
  131.3 4.5 %project.6 = bf16[4,160,256]{2,1,0:T(8,128)(2,1)} custom-call(s32[2]{0:T(128)S(1)} %pad_add_fusion.1.at_ref, bf16[32,80,2048]{2,1,0:T(8,128)(2,1)} %select.15.near_ref, bf16[32,80,2048]{2,1,0:T(8,128)(2,1)} %select.16.far_ref, bf16[16,3,8,80,256]{4,3,2,1,0:T(8,128)(2,1)} %bitcast.44, bf16[4,384,256]{2,1,0:T(8,128)(2,1)} %collective-permute-done.12.mine_ref, ...), custom_call_target="tpu_custom_call" | custom-call | flops 671088640 | bytes 6815744 | tf_op jit(solution)/shard_map/project/pallas_call | solution.py:127
  135.8 4.5 %project.5 = bf16[4,160,256]{2,1,0:T(8,128)(2,1)} custom-call(s32[2]{0:T(128)S(1)} %pad_add_fusion.1.at_ref, bf16[32,80,2048]{2,1,0:T(8,128)(2,1)} %select.15.near_ref, bf16[32,80,2048]{2,1,0:T(8,128)(2,1)} %select.16.far_ref, bf16[16,3,8,80,256]{4,3,2,1,0:T(8,128)(2,1)} %bitcast.45, bf16[4,384,256]{2,1,0:T(8,128)(2,1)} %collective-permute-done.11.mine_ref, ...), custom_call_target="tpu_custom_call" | custom-call | flops 671088640 | bytes 6815744 | tf_op jit(solution)/shard_map/project/pallas_call | solution.py:127
  140.4 2.7 collective-permute-start.19
  143.1 7.1 %project.7 = bf16[8,160,256]{2,1,0:T(8,128)(2,1)} custom-call(s32[2]{0:T(128)S(1)} %get-tuple-element.80.at_ref, bf16[32,80,2048]{2,1,0:T(8,128)(2,1)} %select.15.near_ref, bf16[32,80,2048]{2,1,0:T(8,128)(2,1)} %select.16.far_ref, bf16[16,3,8,80,256]{4,3,2,1,0:T(8,128)(2,1)} %bitcast.46, bf16[8,384,256]{2,1,0:T(8,128)(2,1)S(1)} %collective-permute-done.5.mine_ref, ...), custom_call_target="tpu_custom_call" | custom-call | flops 1342177280 | bytes 13631488 | tf_op jit(solution)/shard_map/project/pallas_call | solution.py:127
  150.2 6.4 %project.8 = bf16[8,160,256]{2,1,0:T(8,128)(2,1)S(1)} custom-call(s32[2]{0:T(128)S(1)} %get-tuple-element.81.at_ref, bf16[32,80,2048]{2,1,0:T(8,128)(2,1)} %select.15.near_ref, bf16[32,80,2048]{2,1,0:T(8,128)(2,1)} %select.16.far_ref, bf16[16,3,8,80,256]{4,3,2,1,0:T(8,128)(2,1)} %bitcast.47, bf16[8,384,256]{2,1,0:T(8,128)(2,1)S(1)} %collective-permute-done.6.mine_ref, ...), custom_call_target="tpu_custom_call" | custom-call | flops 1342177280 | bytes 13631488 | tf_op jit(solution)/shard_map/project/pallas_call | solution.py:127
  156.7 2.7 collective-permute-start.15
  159.4 2.7 collective-permute-start.20
  162.2 6.9 %project.9.refs_0_ = bf16[8,160,256]{2,1,0:T(8,128)(2,1)S(1)} custom-call(s32[2]{0:T(128)S(1)} %pad_add_fusion.at_ref, bf16[32,80,2048]{2,1,0:T(8,128)(2,1)} %select.15.near_ref, bf16[32,80,2048]{2,1,0:T(8,128)(2,1)} %select.16.far_ref, bf16[8,2048,256]{2,1,0:T(8,128)(2,1)} %factor_ref.1), custom_call_target="tpu_custom_call" | custom-call | flops 1342177280 | bytes 13631488 | tf_op jit(solution)/shard_map/project/pallas_call | solution.py:127
  169.1 11.1 %collective-permute-done.18 = bf16[4,160,256]{2,1,0:T(8,128)(2,1)S(1)} collective-permute-done((bf16[4,160,256]{2,1,0:T(8,128)(2,1)S(1)}, bf16[4,160,256]{2,1,0:T(8,128)(2,1)S(1)}, u32[]{:S(2)}, u32[]{:S(2)}) %collective-permute-start.18) | collective-permute-done | bytes 327712 | tf_op jit(solution)/shard_map/ppermute | solution.py:35
  186.0 30.3 %all_to_all.10 = f32[8,192,128]{2,1,0:T(8,128)S(1)} all-to-all(f32[8,192,128]{2,1,0:T(8,128)S(1)} %bitcast.48), channel_id=1, replica_groups=mesh['z'=8,'c'=2,'y'=4,'x'=4] {'z'}, dimensions={0} | all-to-all | bytes 1572864 | tf_op jit(solution)/shard_map/all_to_all | solution.py:353
  216.4 29.4 %all_gather.11 = f32[1536,128]{1,0:T(8,128)S(1)} all-gather(f32[192,128]{1,0:T(8,128)S(1)} %reduce_sum.22), channel_id=1, replica_groups=mesh['z'=8,'c'=2,'y'=4,'x'=4] {'z'}, dimensions={0}, use_global_device_ids=true | all-gather | bytes 884736 | tf_op jit(solution)/shard_map/all_gather | solution.py:354
  245.8 14.2 %factorize.1 = (f32[4,256,256]{2,1,0:T(8,128)S(1)}, bf16[2,4,256,256]{3,2,1,0:T(8,128)(2,1)S(1)}) custom-call(f32[4,3,128,128]{3,2,1,0:T(8,128)S(1)} %bitcast.43), custom_call_target="tpu_custom_call" | custom-call | tf_op jit(solution)/shard_map/factorize/pallas_call | solution.py:253
  261.0 7.1 %collective-permute-start.22 = (bf16[2,4,256,256]{3,2,1,0:T(8,128)(2,1)S(1)}, bf16[2,4,256,256]{3,2,1,0:T(8,128)(2,1)S(1)}, u32[]{:S(2)}, u32[]{:S(2)}) collective-permute-start(bf16[2,4,256,256]{3,2,1,0:T(8,128)(2,1)S(1)} %get-tuple-element.77.mine_ref), channel_id=1, source_target_pairs={{0,16},{16,0},{1,17},{17,1},{2,18},{18,2},{3,19},{19,3},{4,20},{20... | collective-permute-start | bytes 3145736 | tf_op jit(solution)/shard_map/ppermute | solution.py:35
  270.4 3.5 %whiten.1 = bf16[16,320,256]{2,1,0:T(8,128)(2,1)S(1)} custom-call(s32[3]{0:T(128)S(1)} %pad_add_fusion.4.at_ref, bf16[2,4,256,256]{3,2,1,0:T(8,128)(2,1)S(1)} %get-tuple-element.77.mine_ref, bf16[2,4,256,256]{3,2,1,0:T(8,128)(2,1)S(1)} %collective-permute-done.22.other_ref, bf16[8,160,256]{2,1,0:T(8,128)(2,1)S(1)} %project.9.refs_0_, ...), custom_call_target="tpu_custom_call" | custom-call | tf_op jit(solution)/shard_map/whiten/pallas_call | solution.py:297
  275.5 4.4 %all-to-all-start.1 = ((bf16[16,320,256]{2,1,0:T(8,128)(2,1)}), bf16[16,320,256]{2,1,0:T(8,128)(2,1)S(1)}, u32[]{:S(2)}, u32[]{:S(2)}) async-start(bf16[16,320,256]{2,1,0:T(8,128)(2,1)} %copy-done), calls=%async_computation.1 | async-start | bytes 5242880 | tf_op jit(solution)/shard_map/all_to_all | solution.py:446
  283.2 3.8 %maximum_select_fusion = f32[8,256,256]{2,1,0:T(8,128)} fusion(f32[4,256,256]{2,1,0:T(8,128)} %collective-permute-done.23, f32[4,256,256]{2,1,0:T(8,128)} %copy-done.3, pred[]{:T(512)S(6)} %eq.81), kind=kLoop, calls=%fused_computation.3 | loop fusion | flops 1572864 | bytes 4194305 | tf_op jit(solution)/shard_map/jit(_where)/select_n | solution.py:448
  287.0 32.6 %all-to-all-done.1 = bf16[16,320,256]{2,1,0:T(8,128)(2,1)S(1)} async-done(((bf16[16,320,256]{2,1,0:T(8,128)(2,1)}), bf16[16,320,256]{2,1,0:T(8,128)(2,1)S(1)}, u32[]{:S(2)}, u32[]{:S(2)}) %all-to-all-start.1) | async-done | bytes 2621472 | tf_op jit(solution)/shard_map/all_to_all | solution.py:446
  319.6 12.6 %place.1 = bf16[4096,256]{1,0:T(8,128)(2,1)} custom-call(f32[512,8]{1,0:T(8,128)S(1)} %bitcast_add_fusion.slot_ref, bf16[5120,256]{1,0:T(8,128)(2,1)S(1)} %bitcast.42), custom_call_target="tpu_custom_call" | custom-call | tf_op jit(solution)/shard_map/place/pallas_call | solution.py:325
  (99 shorter events, 40.0 us)
Async XLA Ops:
  7.2 9.0 %copy-start.8 = (s32[512,8]{0,1:T(8,128)S(1)}, s32[512,8]{0,1:T(8,128)}, u32[]{:S(2)}) copy-start(s32[512,8]{0,1:T(8,128)} %param.5) | copy-start | bytes 49156
  7.2 9.2 %copy-start.1 = (bf16[512,2048]{1,0:T(8,128)(2,1)S(1)}, bf16[512,2048]{1,0:T(8,128)(2,1)}, u32[]{:S(2)}) copy-start(bf16[512,2048]{1,0:T(8,128)(2,1)} %first_ref.1) | copy-start | bytes 6291460
  7.2 123.0 %all-gather.3.cloned.1.call-start = ((), (), s32[]{:S(2)}) async-start(), calls=%async_computation.2 | async-start | bytes 16711680 | tf_op jit(solution)/shard_map/all_gather | solution.py:384
  8.4 9.6 %collective-permute-start = (bf16[8,80,256]{2,1,0:T(8,128)(2,1)S(1)}, bf16[8,80,256]{2,1,0:T(8,128)(2,1)S(1)}, u32[]{:S(2)}, u32[]{:S(2)}) collective-permute-start(bf16[8,80,256]{2,1,0:T(8,128)(2,1)S(1)} %constant_dynamic-slice_fusion), channel_id=1, source_target_pairs={{0,1},{1,2},{2,3},{3,0},{4,5},{5,6},{6,7},{7,4},{8,9},{9,10},{10,1... | collective-permute-start | bytes 983048 | tf_op jit(solution)/shard_map/ppermute | solution.py:35
  10.5 7.9 %collective-permute-start.1 = (bf16[8,80,256]{2,1,0:T(8,128)(2,1)S(1)}, bf16[8,80,256]{2,1,0:T(8,128)(2,1)S(1)}, u32[]{:S(2)}, u32[]{:S(2)}) collective-permute-start(bf16[8,80,256]{2,1,0:T(8,128)(2,1)S(1)} %constant_dynamic-slice_fusion), channel_id=1, source_target_pairs={{0,3},{1,0},{2,1},{3,2},{4,7},{5,4},{6,5},{7,6},{8,11},{9,8},{10,9... | collective-permute-start | bytes 983048 | tf_op jit(solution)/shard_map/ppermute | solution.py:35
  11.9 15.2 %collective-permute-start.2 = (bf16[8,80,256]{2,1,0:T(8,128)(2,1)S(1)}, bf16[8,80,256]{2,1,0:T(8,128)(2,1)S(1)}, u32[]{:S(2)}, u32[]{:S(2)}) collective-permute-start(bf16[8,80,256]{2,1,0:T(8,128)(2,1)S(1)} %constant_dynamic-slice_fusion), channel_id=1, source_target_pairs={{0,2},{1,3},{2,0},{3,1},{4,6},{5,7},{6,4},{7,5},{8,10},{9,11},{10,... | collective-permute-start | bytes 983048 | tf_op jit(solution)/shard_map/ppermute | solution.py:35
  28.2 35.9 %collective-permute-start.5 = (bf16[8,384,256]{2,1,0:T(8,128)(2,1)}, bf16[8,384,256]{2,1,0:T(8,128)(2,1)S(1)}, u32[]{:S(2)}, u32[]{:S(2)}) collective-permute-start(bf16[8,384,256]{2,1,0:T(8,128)(2,1)} %constant_dynamic-slice_fusion.1), channel_id=1, source_target_pairs={{0,1},{1,2},{2,3},{3,0},{4,5},{5,6},{6,7},{7,4},{8,9},{9,10},{10,1... | collective-permute-start | bytes 4718600 | tf_op jit(solution)/shard_map/ppermute | solution.py:35
  28.6 35.5 %collective-permute-start.6 = (bf16[8,384,256]{2,1,0:T(8,128)(2,1)}, bf16[8,384,256]{2,1,0:T(8,128)(2,1)S(1)}, u32[]{:S(2)}, u32[]{:S(2)}) collective-permute-start(bf16[8,384,256]{2,1,0:T(8,128)(2,1)} %constant_dynamic-slice_fusion.1), channel_id=1, source_target_pairs={{0,3},{1,0},{2,1},{3,2},{4,7},{5,4},{6,5},{7,6},{8,11},{9,8},{10,9... | collective-permute-start | bytes 4718600 | tf_op jit(solution)/shard_map/ppermute | solution.py:35
  30.9 49.5 %collective-permute-start.3 = (bf16[512,2176]{1,0:T(8,128)(2,1)}, bf16[512,2176]{1,0:T(8,128)(2,1)}, u32[]{:S(2)}, u32[]{:S(2)}) collective-permute-start(bf16[512,2176]{1,0:T(8,128)(2,1)} %fusion.1), channel_id=1, source_target_pairs={{0,4},{4,8},{8,12},{12,0},{1,5},{5,9},{9,13},{13,1},{2,6},{6,10},{... | collective-permute-start | bytes 6684680 | tf_op jit(solution)/shard_map/ppermute | solution.py:35
  32.2 48.2 %collective-permute-start.4 = (bf16[512,2176]{1,0:T(8,128)(2,1)}, bf16[512,2176]{1,0:T(8,128)(2,1)}, u32[]{:S(2)}, u32[]{:S(2)}) collective-permute-start(bf16[512,2176]{1,0:T(8,128)(2,1)} %fusion.1), channel_id=1, source_target_pairs={{0,12},{4,0},{8,4},{12,8},{1,13},{5,1},{9,5},{13,9},{2,14},{6,2},{... | collective-permute-start | bytes 6684680 | tf_op jit(solution)/shard_map/ppermute | solution.py:35
  64.1 16.3 %collective-permute-start.7 = (bf16[8,384,256]{2,1,0:T(8,128)(2,1)S(1)}, bf16[8,384,256]{2,1,0:T(8,128)(2,1)}, u32[]{:S(2)}, u32[]{:S(2)}) collective-permute-start(bf16[8,384,256]{2,1,0:T(8,128)(2,1)S(1)} %collective-permute-done.5.mine_ref), channel_id=1, source_target_pairs={{0,16},{16,0},{1,17},{17,1},{2,18},{18,2},{3,19},{19,3},{4,20},{20... | collective-permute-start | bytes 4718600 | tf_op jit(solution)/shard_map/ppermute | solution.py:35
  66.5 13.9 %collective-permute-start.8 = (bf16[8,384,256]{2,1,0:T(8,128)(2,1)S(1)}, bf16[8,384,256]{2,1,0:T(8,128)(2,1)}, u32[]{:S(2)}, u32[]{:S(2)}) collective-permute-start(bf16[8,384,256]{2,1,0:T(8,128)(2,1)S(1)} %collective-permute-done.6.mine_ref), channel_id=1, source_target_pairs={{0,16},{16,0},{1,17},{17,1},{2,18},{18,2},{3,19},{19,3},{4,20},{20... | collective-permute-start | bytes 4718600 | tf_op jit(solution)/shard_map/ppermute | solution.py:35
  82.8 24.6 %collective-permute-start.10 = (bf16[256,2176]{1,0:T(8,128)(2,1)}, bf16[256,2176]{1,0:T(8,128)(2,1)}, u32[]{:S(2)}, u32[]{:S(2)}) collective-permute-start(bf16[256,2176]{1,0:T(8,128)(2,1)} %slice.26), channel_id=1, source_target_pairs={{0,12},{4,0},{8,4},{12,8},{1,13},{5,1},{9,5},{13,9},{2,14},{6,2},{... | collective-permute-start | bytes 3342344 | tf_op jit(solution)/shard_map/ppermute | solution.py:35
  87.4 24.1 %collective-permute-start.9 = (bf16[256,2176]{1,0:T(8,128)(2,1)}, bf16[256,2176]{1,0:T(8,128)(2,1)}, u32[]{:S(2)}, u32[]{:S(2)}) collective-permute-start(bf16[256,2176]{1,0:T(8,128)(2,1)} %slice.25), channel_id=1, source_target_pairs={{0,4},{4,8},{8,12},{12,0},{1,5},{5,9},{9,13},{13,1},{2,6},{6,10},{... | collective-permute-start | bytes 3342344 | tf_op jit(solution)/shard_map/ppermute | solution.py:35
  89.1 4.9 %copy-start.9 = (s32[512,8]{0,1:T(8,128)S(1)}, s32[512,8]{0,1:T(8,128)}, u32[]{:S(2)}) copy-start(s32[512,8]{0,1:T(8,128)} %param.5) | copy-start | bytes 49156
  89.1 4.9 %copy-start.11 = (s32[1,512,8]{1,2,0:T(8,128)S(1)}, s32[1,512,8]{1,2,0:T(8,128)}, u32[]{:S(2)}) copy-start(s32[1,512,8]{1,2,0:T(8,128)} %copy.27) | copy-start | bytes 49156
  90.1 17.0 %collective-permute-start.11 = (bf16[4,384,256]{2,1,0:T(8,128)(2,1)}, bf16[4,384,256]{2,1,0:T(8,128)(2,1)}, u32[]{:S(2)}, u32[]{:S(2)}) collective-permute-start(bf16[4,384,256]{2,1,0:T(8,128)(2,1)} %slice.27), channel_id=1, source_target_pairs={{0,1},{1,2},{2,3},{3,0},{4,5},{5,6},{6,7},{7,4},{8,9},{9,10},{10,1... | collective-permute-start | bytes 2359304 | tf_op jit(solution)/shard_map/ppermute | solution.py:35
  91.1 16.3 %collective-permute-start.12 = (bf16[4,384,256]{2,1,0:T(8,128)(2,1)}, bf16[4,384,256]{2,1,0:T(8,128)(2,1)}, u32[]{:S(2)}, u32[]{:S(2)}) collective-permute-start(bf16[4,384,256]{2,1,0:T(8,128)(2,1)} %slice.28), channel_id=1, source_target_pairs={{0,3},{1,0},{2,1},{3,2},{4,7},{5,4},{6,5},{7,6},{8,11},{9,8},{10,9... | collective-permute-start | bytes 2359304 | tf_op jit(solution)/shard_map/ppermute | solution.py:35
  113.3 15.1 %collective-permute-start.13 = (bf16[4,384,256]{2,1,0:T(8,128)(2,1)}, bf16[4,384,256]{2,1,0:T(8,128)(2,1)S(1)}, u32[]{:S(2)}, u32[]{:S(2)}) collective-permute-start(bf16[4,384,256]{2,1,0:T(8,128)(2,1)} %collective-permute-done.11.mine_ref), channel_id=1, source_target_pairs={{0,16},{16,0},{1,17},{17,1},{2,18},{18,2},{3,19},{19,3},{4,20},{20... | collective-permute-start | bytes 2359304 | tf_op jit(solution)/shard_map/ppermute | solution.py:35
  117.8 11.5 %collective-permute-start.14 = (bf16[4,384,256]{2,1,0:T(8,128)(2,1)}, bf16[4,384,256]{2,1,0:T(8,128)(2,1)S(1)}, u32[]{:S(2)}, u32[]{:S(2)}) collective-permute-start(bf16[4,384,256]{2,1,0:T(8,128)(2,1)} %collective-permute-done.12.mine_ref), channel_id=1, source_target_pairs={{0,16},{16,0},{1,17},{17,1},{2,18},{18,2},{3,19},{19,3},{4,20},{20... | collective-permute-start | bytes 2359304 | tf_op jit(solution)/shard_map/ppermute | solution.py:35
  131.3 4.5 %copy-start.5 = (bf16[4,384,256]{2,1,0:T(8,128)(2,1)S(1)}, bf16[4,384,256]{2,1,0:T(8,128)(2,1)}, u32[]{:S(2)}) copy-start(bf16[4,384,256]{2,1,0:T(8,128)(2,1)} %copy-done.4) | copy-start | bytes 2359300
  140.3 19.1 %collective-permute-start.17 = (bf16[4,160,256]{2,1,0:T(8,128)(2,1)}, bf16[4,160,256]{2,1,0:T(8,128)(2,1)S(1)}, u32[]{:S(2)}, u32[]{:S(2)}) collective-permute-start(bf16[4,160,256]{2,1,0:T(8,128)(2,1)} %project.5), channel_id=1, source_target_pairs={{0,1},{1,2},{2,3},{3,0},{4,5},{5,6},{6,7},{7,4},{8,9},{9,10},{10,1... | collective-permute-start | bytes 983048 | tf_op jit(solution)/shard_map/ppermute | solution.py:35
  140.4 19.1 %collective-permute-start.19 = (bf16[4,160,256]{2,1,0:T(8,128)(2,1)}, bf16[4,160,256]{2,1,0:T(8,128)(2,1)}, u32[]{:S(2)}, u32[]{:S(2)}) collective-permute-start(bf16[4,160,256]{2,1,0:T(8,128)(2,1)} %project.6), channel_id=1, source_target_pairs={{0,3},{1,0},{2,1},{3,2},{4,7},{5,4},{6,5},{7,6},{8,11},{9,8},{10,9... | collective-permute-start | bytes 983048 | tf_op jit(solution)/shard_map/ppermute | solution.py:35
  156.6 23.6 %collective-permute-start.16 = (bf16[8,160,256]{2,1,0:T(8,128)(2,1)S(1)}, bf16[8,160,256]{2,1,0:T(8,128)(2,1)S(1)}, u32[]{:S(2)}, u32[]{:S(2)}) collective-permute-start(bf16[8,160,256]{2,1,0:T(8,128)(2,1)S(1)} %project.8), channel_id=1, source_target_pairs={{0,1},{1,2},{2,3},{3,0},{4,5},{5,6},{6,7},{7,4},{8,9},{9,10},{10,1... | collective-permute-start | bytes 1966088 | tf_op jit(solution)/shard_map/ppermute | solution.py:35
  156.7 23.6 %collective-permute-start.15 = (bf16[8,160,256]{2,1,0:T(8,128)(2,1)}, bf16[8,160,256]{2,1,0:T(8,128)(2,1)S(1)}, u32[]{:S(2)}, u32[]{:S(2)}) collective-permute-start(bf16[8,160,256]{2,1,0:T(8,128)(2,1)} %project.7), channel_id=1, source_target_pairs={{0,3},{1,0},{2,1},{3,2},{4,7},{5,4},{6,5},{7,6},{8,11},{9,8},{10,9... | collective-permute-start | bytes 1966088 | tf_op jit(solution)/shard_map/ppermute | solution.py:35
  159.4 20.8 %collective-permute-start.18 = (bf16[4,160,256]{2,1,0:T(8,128)(2,1)S(1)}, bf16[4,160,256]{2,1,0:T(8,128)(2,1)S(1)}, u32[]{:S(2)}, u32[]{:S(2)}) collective-permute-start(bf16[4,160,256]{2,1,0:T(8,128)(2,1)S(1)} %collective-permute-done.17), channel_id=1, source_target_pairs={{0,1},{1,2},{2,3},{3,0},{4,5},{5,6},{6,7},{7,4},{8,9},{9,10},{10,1... | collective-permute-start | bytes 983048 | tf_op jit(solution)/shard_map/ppermute | solution.py:35
  159.4 20.8 %collective-permute-start.20 = (bf16[4,160,256]{2,1,0:T(8,128)(2,1)}, bf16[4,160,256]{2,1,0:T(8,128)(2,1)S(1)}, u32[]{:S(2)}, u32[]{:S(2)}) collective-permute-start(bf16[4,160,256]{2,1,0:T(8,128)(2,1)} %collective-permute-done.19), channel_id=1, source_target_pairs={{0,3},{1,0},{2,1},{3,2},{4,7},{5,4},{6,5},{7,6},{8,11},{9,8},{10,9... | collective-permute-start | bytes 983048 | tf_op jit(solution)/shard_map/ppermute | solution.py:35
  182.0 3.9 %collective-permute-start.21 = (f32[4,3,128,128]{3,2,1,0:T(8,128)S(1)}, f32[4,3,128,128]{3,2,1,0:T(8,128)S(1)}, u32[]{:S(2)}, u32[]{:S(2)}) collective-permute-start(f32[4,3,128,128]{3,2,1,0:T(8,128)S(1)} %get-tuple-element.75), channel_id=1, source_target_pairs={{0,16},{16,0},{1,17},{17,1},{2,18},{18,2},{3,19},{19,3},{4,20},{20... | collective-permute-start | bytes 2359304 | tf_op jit(solution)/shard_map/ppermute | solution.py:35
  261.0 9.4 %collective-permute-start.22 = (bf16[2,4,256,256]{3,2,1,0:T(8,128)(2,1)S(1)}, bf16[2,4,256,256]{3,2,1,0:T(8,128)(2,1)S(1)}, u32[]{:S(2)}, u32[]{:S(2)}) collective-permute-start(bf16[2,4,256,256]{3,2,1,0:T(8,128)(2,1)S(1)} %get-tuple-element.77.mine_ref), channel_id=1, source_target_pairs={{0,16},{16,0},{1,17},{17,1},{2,18},{18,2},{3,19},{19,3},{4,20},{20... | collective-permute-start | bytes 3145736 | tf_op jit(solution)/shard_map/ppermute | solution.py:35
  275.4 5.1 %copy-start.10 = (s32[512,8]{0,1:T(8,128)S(1)}, s32[512,8]{0,1:T(8,128)}, u32[]{:S(2)}) copy-start(s32[512,8]{0,1:T(8,128)} %param.5) | copy-start | bytes 49156
  275.5 44.1 %all-to-all-start.1 = ((bf16[16,320,256]{2,1,0:T(8,128)(2,1)}), bf16[16,320,256]{2,1,0:T(8,128)(2,1)S(1)}, u32[]{:S(2)}, u32[]{:S(2)}) async-start(bf16[16,320,256]{2,1,0:T(8,128)(2,1)} %copy-done), calls=%async_computation.1 | async-start | bytes 5242880 | tf_op jit(solution)/shard_map/all_to_all | solution.py:446
  279.8 3.4 collective-permute-start.23
  (6 other events, 7.0 us)
Sparse Core Ops, SparseCore 0:
  28.3 93.6 all-gather.2
